TPU v7x, 128 devices: a whole 4x4x4 slice. The times are simulated.
128 devices in a mesh: gy: 16 (over x_hi, z, core), gx: 4 (over y), tp: 2 (over x_lo).
Axes of the slice: x: 4 (x_hi: 2, x_lo: 2; x = x_hi * 2 + x_lo), y: 4, z: 4, core: 2. Of those that a mesh axis runs over, the one named last changes fastest.
Arguments:
- features: float32 [4, 256, 64, 1536], P(None, 'gy', 'gx')
- qkv_weight: bfloat16 [2, 1536, 3, 1536], P(None, None, None, 'tp')
- out_weight: bfloat16 [2, 1536, 1536], P(None, 'tp'), may hold values from -0.15625 to 0.15625
- norm_gain: float32 [2, 1536], replicated, may hold values from 0.5 to 1.5
- layer_scale: float32 [2, 1536], replicated, may hold values from 0.5 to 2
- valid_counts: int32 [16, 4], replicated, may hold values from 137 to 256, as said below
Outputs:
- blended: float32 [4, 256, 64, 1536], P(None, 'gy', 'gx')
Inputs may be any that keep to these rules, and one draw needn't show every extreme that they name: `valid_counts`: every tile is valid from its first patch in row-major order up to its count; some tile is complete.
All inputs are finite; a program needn't handle non-finite values.
Results may differ from a plain program's by a relative error of at most 0.009.
Values may be sent and summed in bfloat16 or wider, within the bound.
A program may use at most 128 MiB of HBM per device.

v0:
```python
import jax
import jax.numpy as jnp
from jax import lax
from jax.sharding import PartitionSpec as P

HD = 64


def passed_along(block, axis, distance):
    devices = range(lax.axis_size(axis))
    route = [(i - distance, i) for i in devices if i - distance in devices]
    return lax.ppermute(block, axis, route)


def for_sending(x):

    def short(part):
        return part.astype(jnp.bfloat16) if part.dtype == jnp.float32 else part

    return jax.tree.map(short, x)


def normalize(values, gain_row):
    average = jnp.mean(values, axis=-1, keepdims=True)
    centred = values - average
    spread = jnp.mean(centred * centred, axis=-1, keepdims=True)
    return (centred * lax.rsqrt(spread + 1e-06) * gain_row).astype(jnp.bfloat16)


def attend(normed, valid, qkv_w):
    images, length, channels = normed.shape
    inner = qkv_w.shape[-1]
    packed = jnp.dot(
        normed.reshape(-1, channels),
        qkv_w.reshape(channels, -1),
        preferred_element_type=jnp.float32,
    ).astype(jnp.bfloat16)
    packed = packed.reshape(images, length, 3, inner // HD, HD)
    query_part = packed[:, :, 0]
    key_part = packed[:, :, 1]
    value_part = packed[:, :, 2]
    scores = jnp.einsum(
        "bqhe,bkhe->bhqk", query_part, key_part, preferred_element_type=jnp.float32
    ) * HD ** (-0.5)
    scores = jnp.where(valid[None, None, None, :], scores, -1e30)
    largest = jnp.max(scores, axis=-1, keepdims=True)
    powers = jnp.exp(scores - largest)
    totals = jnp.sum(powers, axis=-1, keepdims=True)
    attn_prob = (powers / totals).astype(jnp.bfloat16)
    head_out = jnp.einsum(
        "bhqk,bkhe->bqhe", attn_prob, value_part, preferred_element_type=jnp.float32
    )
    return head_out.reshape(images, length, inner).astype(jnp.bfloat16)


def project(head_out, proj):
    flat = head_out.reshape(-1, head_out.shape[-1])
    partial_out = jnp.dot(flat, proj, preferred_element_type=jnp.float32)
    return lax.psum(partial_out.astype(jnp.bfloat16), "tp").astype(jnp.float32)


def blend_weight(tile_rows, tile_cols):
    row_part = jnp.sin(jnp.pi * (jnp.arange(tile_rows, dtype=jnp.float32) + 0.5) / tile_rows) ** 2
    col_part = jnp.sin(jnp.pi * (jnp.arange(tile_cols, dtype=jnp.float32) + 0.5) / tile_cols) ** 2
    return (0.25 + 0.75 * row_part[:, None] * col_part[None, :])[:, :, None]


def shards(features, qkv_weight, out_weight, norm_gain, layer_scale, valid_counts):
    images, tile_rows, tile_cols, channels = features.shape
    grid_rows = lax.axis_size("gy")
    grid_cols = lax.axis_size("gx")
    row_id = lax.axis_index("gy")
    col_id = lax.axis_index("gx")
    local_r = jnp.arange(tile_rows, dtype=jnp.int32)[:, None]
    local_c = jnp.arange(tile_cols, dtype=jnp.int32)[None, :]
    position = local_r * tile_cols + local_c
    own_valid = (position < valid_counts[row_id, col_id]).reshape(-1)
    normed = normalize(features, norm_gain[0]).reshape(images, tile_rows * tile_cols, channels)
    head_out = attend(normed, own_valid, qkv_weight[0])
    summed = project(head_out, out_weight[0]).reshape(features.shape)
    after_first = features + layer_scale[0] * summed
    second_in = normalize(after_first, norm_gain[1])
    from_right = passed_along(second_in[:, :, : tile_cols // 2], "gx", -1)
    row_band = jnp.concatenate([second_in[:, :, tile_cols // 2 :], from_right], axis=2)
    from_below = passed_along(row_band[:, : tile_rows // 2], "gy", -1)
    shifted = jnp.concatenate([row_band[:, tile_rows // 2 :], from_below], axis=1)
    shifted_r = local_r + tile_rows // 2
    shifted_c = local_c + tile_cols // 2
    source_r = row_id + shifted_r // tile_rows
    source_c = col_id + shifted_c // tile_cols
    inside = (source_r < grid_rows) & (source_c < grid_cols)
    tile_count = valid_counts[
        jnp.minimum(source_r, grid_rows - 1), jnp.minimum(source_c, grid_cols - 1)
    ]
    crop_valid = (
        inside & (shifted_r % tile_rows * tile_cols + shifted_c % tile_cols < tile_count)
    ).reshape(-1)
    crop_heads = attend(
        shifted.reshape(images, tile_rows * tile_cols, channels), crop_valid, qkv_weight[1]
    )
    blend_map = blend_weight(tile_rows, tile_cols)
    summed = project(crop_heads, out_weight[1]).reshape(features.shape)
    change = layer_scale[1] * blend_map * summed
    from_above = passed_along(change[:, tile_rows // 2 :].astype(jnp.bfloat16), "gy", 1).astype(
        jnp.float32
    )
    band_back = jnp.concatenate([from_above, change[:, : tile_rows // 2]], axis=1)
    from_left = passed_along(for_sending(band_back[:, :, tile_cols // 2 :]), "gx", 1)
    update = jnp.concatenate([from_left, band_back[:, :, : tile_cols // 2]], axis=2)
    return after_first + update


def solution(mesh):
    in_specs = (
        P(None, "gy", "gx", None),
        P(None, None, None, "tp"),
        P(None, "tp", None),
        P(),
        P(),
        P(),
    )
    out_specs = P(None, "gy", "gx", None)
    return jax.shard_map(shards, mesh=mesh, in_specs=in_specs, out_specs=out_specs, check_vma=False)
```

profile of v0, /device:TPU:6, one launch (start us, length us, event | category | flops | bytes accessed | tf_op | source)
XLA Modules:
  0.0 480.1 jit_solution(16469693757017490457)
XLA Ops:
  6.5 0.8 slice_reduce_fusion.2
  7.4 3.1 reduce_sum.54
  10.5 3.5 multiply_reduce_fusion.1
  14.1 10.1 %fusion.37 = (bf16[1,1536,3,768]{3,1,2,0:T(8,128)(2,1)}, bf16[1,1536,3,768]{3,1,2,0:T(8,128)(2,1)}) fusion(bf16[2,1536,3,768]{3,1,2,0:T(8,128)(2,1)} %param.7), kind=kLoop, calls=%fused_computation.95 | loop fusion | bytes 28311552 | tf_op jit(solution)/shard_map/slice | solution.py:99
  24.1 10.3 %copy.31 = bf16[1,1536,3,768]{1,3,2,0:T(8,128)(2,1)} copy(bf16[1,1536,3,768]{3,1,2,0:T(8,128)(2,1)} %get-tuple-element.10) | data formatting | bytes 14155776
  34.4 3.8 multiply_convert_fusion.1
  38.2 1.0 copy-done.2
  39.2 9.1 %convolution_convert_fusion.1 = bf16[1024,2304]{1,0:T(8,128)(2,1)} fusion(bf16[1024,1536]{1,0:T(8,128)(2,1)S(1)} %bitcast.72, bf16[1536,2304]{0,1:T(8,128)(2,1)S(1)} %bitcast.66), kind=kOutput, calls=%fused_computation.31 | convolution fusion | flops 7250116608 | bytes 14942208 | tf_op jit(solution)/shard_map/dot_general | solution.py:33
  48.3 6.7 %copy.16 = bf16[1024,2304]{0,1:T(8,128)(2,1)} copy(bf16[1024,2304]{1,0:T(8,128)(2,1)} %convolution_convert_fusion.1) | data formatting | bytes 9437184 | tf_op jit(solution)/shard_map/convert_element_type | solution.py:37
  55.0 8.9 %reshape.304 = bf16[4,256,3,12,64]{1,0,4,3,2:T(4,128)(2,1)} reshape(bf16[1024,2304]{0,1:T(8,128)(2,1)} %copy.16) | data formatting | bytes 9437184 | tf_op jit(solution)/shard_map/reshape | solution.py:38
  63.9 4.5 fusion.39
  68.4 0.6 dynamic_slice.3
  69.0 0.7 add_compare_fusion.1
  69.8 1.8 fusion.24
  71.6 7.9 %fusion.41 = (f32[4,12,256]{2,1,0:T(8,128)S(1)}, f32[4,12,256,256]{2,3,1,0:T(8,128)}) fusion(f32[4,12,256,256]{2,3,1,0:T(8,128)S(1)} %fusion.24, pred[256]{0:T(512)(128)(4,1)S(1)} %lt.72), kind=kOutput, calls=%fused_computation.99 | output fusion | flops 18874624 | bytes 25215232 | tf_op jit(solution)/shard_map/sub | solution.py:47
  79.6 5.8 %fusion.25 = bf16[4,256,12,64]{1,3,2,0:T(8,128)(2,1)S(1)} fusion(f32[4,12,256,256]{2,3,1,0:T(8,128)} %get-tuple-element.22, f32[4,12,256]{2,1,0:T(8,128)S(1)} %get-tuple-element.21, bf16[4,256,1,12,64]{1,0,4,3,2:T(4,128)(2,1)S(1)} %copy-done.3), kind=kOutput, calls=%fused_computation.56 | convolution fusion | flops 409731072 | bytes 15777792 | tf_op jit(solution)/shard_map/bhqk,bkhe->bqhe/dot_general | solution.py:50
  85.4 1.2 copy.21
  87.0 4.3 convolution_convert_fusion.3
  91.4 0.6 copy-done.4
  92.0 93.5 %all-reduce.3.cloned.1.call-done = bf16[4,16,16,1536]{3,2,1,0:T(8,128)(2,1)} async-done(((bf16[4,16,16,1536]{3,2,1,0:T(8,128)(2,1)}), bf16[4,16,16,1536]{3,2,1,0:T(8,128)(2,1)}) %all-reduce.3.cloned.1.call-update) | async-done | bytes 3145744 | tf_op jit(solution)/shard_map/psum | solution.py:59
  185.5 4.7 fusion.36
  190.3 4.3 multiply_reduce_fusion
  194.7 1.6 multiply_convert_fusion
  196.4 1.3 collective-permute-start
  197.7 36.7 %collective-permute-done = bf16[4,16,8,1536]{3,2,1,0:T(8,128)(2,1)S(1)} collective-permute-done((bf16[4,16,8,1536]{3,2,1,0:T(8,128)(2,1)S(1)}, bf16[4,16,8,1536]{3,2,1,0:T(8,128)(2,1)S(1)}, u32[]{:S(2)}, u32[]{:S(2)}) %collective-permute-start) | collective-permute-done | bytes 1572896 | tf_op jit(solution)/shard_map/ppermute | solution.py:12
  234.5 2.1 fusion.22
  236.5 4.0 collective-permute-start.1
  240.5 10.2 %copy.35 = bf16[1,1536,3,768]{1,3,2,0:T(8,128)(2,1)} copy(bf16[1,1536,3,768]{3,1,2,0:T(8,128)(2,1)} %get-tuple-element.9) | data formatting | bytes 14155776
  250.9 2.4 gather_fusion
  253.6 5.2 %collective-permute-done.1 = bf16[4,8,16,1536]{3,2,1,0:T(8,128)(2,1)} collective-permute-done((bf16[4,8,16,1536]{3,2,1,0:T(8,128)(2,1)}, bf16[4,8,16,1536]{3,2,1,0:T(8,128)(2,1)}, u32[]{:S(2)}, u32[]{:S(2)}) %collective-permute-start.1) | collective-permute-done | bytes 1572896 | tf_op jit(solution)/shard_map/ppermute | solution.py:12
  258.8 2.2 pad_maximum_fusion.1
  260.9 12.2 %convolution_convert_fusion = bf16[1024,2304]{1,0:T(8,128)(2,1)} fusion(bf16[1024,1536]{1,0:T(8,128)(2,1)S(1)} %bitcast.71, bf16[1536,2304]{0,1:T(8,128)(2,1)} %bitcast.65), kind=kOutput, calls=%fused_computation.30 | convolution fusion | flops 7250116608 | bytes 14942208 | tf_op jit(solution)/shard_map/dot_general | solution.py:33
  273.1 6.6 %copy.23 = bf16[1024,2304]{0,1:T(8,128)(2,1)} copy(bf16[1024,2304]{1,0:T(8,128)(2,1)} %convolution_convert_fusion) | data formatting | bytes 9437184 | tf_op jit(solution)/shard_map/convert_element_type | solution.py:37
  279.7 8.9 %reshape.307 = bf16[4,256,3,12,64]{1,0,4,3,2:T(4,128)(2,1)} reshape(bf16[1024,2304]{0,1:T(8,128)(2,1)} %copy.23) | data formatting | bytes 9437184 | tf_op jit(solution)/shard_map/reshape | solution.py:38
  288.6 3.3 fusion.38
  291.8 1.8 fusion.23
  293.7 7.9 %fusion.42 = (f32[4,12,256]{2,1,0:T(8,128)S(1)}, f32[4,12,256,256]{2,3,1,0:T(8,128)}) fusion(f32[4,12,256,256]{2,3,1,0:T(8,128)S(1)} %fusion.23, pred[256]{0:T(512)(128)(4,1)S(1)} %and.102), kind=kOutput, calls=%fused_computation.100 | output fusion | flops 18874624 | bytes 25215232 | tf_op jit(solution)/shard_map/sub | solution.py:47
  301.6 5.8 %fusion.26 = bf16[4,256,12,64]{1,3,2,0:T(8,128)(2,1)S(1)} fusion(f32[4,12,256,256]{2,3,1,0:T(8,128)} %get-tuple-element.24, f32[4,12,256]{2,1,0:T(8,128)S(1)} %get-tuple-element.23, bf16[4,256,1,12,64]{1,0,4,3,2:T(4,128)(2,1)S(1)} %get-tuple-element.11), kind=kOutput, calls=%fused_computation.57 | convolution fusion | flops 409731072 | bytes 15777792 | tf_op jit(solution)/shard_map/bhqk,bkhe->bqhe/dot_general | solution.py:50
  307.5 1.2 copy.28
  309.1 4.3 convolution_convert_fusion.2
  313.5 1.3 broadcast_multiply_fusion
  314.9 91.7 %all-reduce.5.cloned.1.call-done = bf16[4,16,16,1536]{3,2,1,0:T(8,128)(2,1)} async-done(((bf16[4,16,16,1536]{3,2,1,0:T(8,128)(2,1)}), bf16[4,16,16,1536]{3,2,1,0:T(8,128)(2,1)}) %all-reduce.5.cloned.1.call-update) | async-done | bytes 3145744 | tf_op jit(solution)/shard_map/psum | solution.py:59
  406.5 3.3 convert_multiply_fusion
  410.1 1.9 collective-permute-start.2
  412.3 23.1 %collective-permute-done.2 = bf16[4,8,16,1536]{3,2,1,0:T(8,128)(2,1)S(1)} collective-permute-done((bf16[4,8,16,1536]{3,2,1,0:T(8,128)(2,1)S(1)}, bf16[4,8,16,1536]{3,2,1,0:T(8,128)(2,1)S(1)}, u32[]{:S(2)}, u32[]{:S(2)}) %collective-permute-start.2) | collective-permute-done | bytes 1572896 | tf_op jit(solution)/shard_map/ppermute | solution.py:12
  436.0 3.8 collective-permute-start.3
  439.8 29.3 %collective-permute-done.3 = bf16[4,16,8,1536]{3,2,1,0:T(8,128)(2,1)S(1)} collective-permute-done((bf16[4,16,8,1536]{3,2,1,0:T(8,128)(2,1)S(1)}, bf16[4,16,8,1536]{3,2,1,0:T(8,128)(2,1)S(1)}, u32[]{:S(2)}, u32[]{:S(2)}) %collective-permute-start.3) | collective-permute-done | bytes 1572896 | tf_op jit(solution)/shard_map/ppermute | solution.py:12
  469.5 3.7 fusion.5
  (57 shorter events, 3.3 us)
Async XLA Ops:
  6.5 179.0 %all-reduce.3.cloned.1.call-start = ((), (), s32[]{:S(2)}) async-start(), calls=%async_computation | async-start | bytes 6291456 | tf_op jit(solution)/shard_map/psum | solution.py:59
  34.4 4.8 %copy-start.2 = (bf16[1,1536,3,768]{1,3,2,0:T(8,128)(2,1)S(1)}, bf16[1,1536,3,768]{1,3,2,0:T(8,128)(2,1)}, u32[]{:S(2)}) copy-start(bf16[1,1536,3,768]{1,3,2,0:T(8,128)(2,1)} %copy.31) | copy-start | bytes 21233668
  63.9 4.5 copy-start
  71.6 8.0 %copy-start.3 = (bf16[4,256,1,12,64]{1,0,4,3,2:T(4,128)(2,1)S(1)}, bf16[4,256,1,12,64]{1,0,4,3,2:T(4,128)(2,1)}, u32[]{:S(2)}) copy-start(bf16[4,256,1,12,64]{1,0,4,3,2:T(4,128)(2,1)} %get-tuple-element.14) | copy-start | bytes 4718596
  79.6 7.4 %slice-start.4 = ((s8[4718592]{0:T(1024)(128)(4,1)}), s8[4194304]{0:T(1024)(128)(4,1)S(1)}, s32[]{:S(2)}) async-start(s8[4718592]{0:T(1024)(128)(4,1)} %bitcast.75), calls=%async_computation.6 | async-start | bytes 8388608
  79.6 7.5 %slice-start.5 = ((s8[4718592]{0:T(1024)(128)(4,1)}), s8[524288]{0:T(1024)(128)(4,1)S(1)}, s32[]{:S(2)}) async-start(s8[4718592]{0:T(1024)(128)(4,1)} %bitcast.75), calls=%async_computation.7 | async-start | bytes 1048576
  91.3 0.7 copy-start.4
  91.3 315.2 %all-reduce.5.cloned.1.call-start = ((), (), s32[]{:S(2)}) async-start(), calls=%async_computation.1 | async-start | bytes 6291456 | tf_op jit(solution)/shard_map/psum | solution.py:59
  185.5 4.8 copy-start.1
  185.5 9.1 %slice-start = ((s8[6291456]{0:T(1024)(128)(4,1)}), s8[4194304]{0:T(1024)(128)(4,1)S(1)}, s32[]{:S(2)}) async-start(s8[6291456]{0:T(1024)(128)(4,1)} %bitcast.61), calls=%async_computation.2 | async-start | bytes 8388608
  190.3 4.4 slice-start.1
  196.4 38.0 %collective-permute-start = (bf16[4,16,8,1536]{3,2,1,0:T(8,128)(2,1)S(1)}, bf16[4,16,8,1536]{3,2,1,0:T(8,128)(2,1)S(1)}, u32[]{:S(2)}, u32[]{:S(2)}) collective-permute-start(bf16[4,16,8,1536]{3,2,1,0:T(8,128)(2,1)S(1)} %get-tuple-element.20), channel_id=1, source_target_pairs={{2,0},{4,2},{6,4},{3,1},{5,3},{7,5},{10,8},{12,10},{14,12},{11,9},... | collective-permute-start | bytes 4718600 | tf_op jit(solution)/shard_map/ppermute | solution.py:12
  236.5 22.2 %collective-permute-start.1 = (bf16[4,8,16,1536]{3,2,1,0:T(8,128)(2,1)}, bf16[4,8,16,1536]{3,2,1,0:T(8,128)(2,1)}, u32[]{:S(2)}, u32[]{:S(2)}) collective-permute-start(bf16[4,8,16,1536]{3,2,1,0:T(8,128)(2,1)} %get-tuple-element.18), channel_id=1, source_target_pairs={{8,0},{16,8},{24,16},{32,24},{40,32},{48,40},{56,48},{64,56},{72,6... | collective-permute-start | bytes 4718600 | tf_op jit(solution)/shard_map/ppermute | solution.py:12
  301.6 7.4 %slice-start.6 = ((s8[4718592]{0:T(1024)(128)(4,1)}), s8[4194304]{0:T(1024)(128)(4,1)S(1)}, s32[]{:S(2)}) async-start(s8[4718592]{0:T(1024)(128)(4,1)} %bitcast.77), calls=%async_computation.8 | async-start | bytes 8388608
  301.6 7.5 %slice-start.7 = ((s8[4718592]{0:T(1024)(128)(4,1)}), s8[524288]{0:T(1024)(128)(4,1)S(1)}, s32[]{:S(2)}) async-start(s8[4718592]{0:T(1024)(128)(4,1)} %bitcast.77), calls=%async_computation.9 | async-start | bytes 1048576
  410.1 25.3 %collective-permute-start.2 = (bf16[4,8,16,1536]{3,2,1,0:T(8,128)(2,1)S(1)}, bf16[4,8,16,1536]{3,2,1,0:T(8,128)(2,1)S(1)}, u32[]{:S(2)}, u32[]{:S(2)}) collective-permute-start(bf16[4,8,16,1536]{3,2,1,0:T(8,128)(2,1)S(1)} %slice.133), channel_id=1, source_target_pairs={{0,8},{8,16},{16,24},{24,32},{32,40},{40,48},{48,56},{56,64},{64,7... | collective-permute-start | bytes 4718600 | tf_op jit(solution)/shard_map/ppermute | solution.py:12
  435.4 34.0 %slice-start.2 = ((s8[6291456]{0:T(1024)(128)(4,1)}), s8[4194304]{0:T(1024)(128)(4,1)S(1)}, s32[]{:S(2)}) async-start(s8[6291456]{0:T(1024)(128)(4,1)} %bitcast.63), calls=%async_computation.4 | async-start | bytes 8388608
  435.8 33.7 %slice-start.3 = ((s8[6291456]{0:T(1024)(128)(4,1)}), s8[2097152]{0:T(1024)(128)(4,1)S(1)}, s32[]{:S(2)}) async-start(s8[6291456]{0:T(1024)(128)(4,1)} %bitcast.63), calls=%async_computation.5 | async-start | bytes 4194304
  436.0 33.0 %collective-permute-start.3 = (bf16[4,16,8,1536]{3,2,1,0:T(8,128)(2,1)S(1)}, bf16[4,16,8,1536]{3,2,1,0:T(8,128)(2,1)S(1)}, u32[]{:S(2)}, u32[]{:S(2)}) collective-permute-start(bf16[4,16,8,1536]{3,2,1,0:T(8,128)(2,1)S(1)} %fusion.15), channel_id=1, source_target_pairs={{0,2},{2,4},{4,6},{1,3},{3,5},{5,7},{8,10},{10,12},{12,14},{9,11},... | collective-permute-start | bytes 4718600 | tf_op jit(solution)/shard_map/ppermute | solution.py:12
Sparse Core Ops, SparseCore 0:
  91.4 94.0 all-reduce.2
  313.5 92.9 all-reduce.4
where the time goes:
time: 483 us; the launch traced here: 480 us
  waiting for transfers between devices  279 us (58%)
  local copies, waits for them, and re-layouts  79.2 us (16%)
  other arithmetic  51.5 us (11%)
  matrix products  45.1 us (9%)
  between operations  13.8 us (3%)
  starting transfers between devices  11 us (2%)
    psum x2, waiting for transfers between devices, project(): return lax.psum(partial_out.astype(jnp.bfloat16), 'tp').astype(jnp.float32)  185 us
    ppermute x4, waiting for transfers between devices, passed_along(): return lax.ppermute(block, axis, route)  94.2 us
    unnamed x30, local copies, waits for them, and re-layouts  22.9 us
    dot_general x2, matrix products, attend(): jnp.dot(normed.reshape(-1, channels), qkv_w.reshape(channels, -1), prefer...  21.2 us
    reshape x2, local copies, waits for them, and re-layouts, attend(): packed = packed.reshape(images, length, 3, inner // HD, HD)  17.7 us
    sub x2, other arithmetic, attend(): powers = jnp.exp(scores - largest)  15.9 us
    convert_element_type x2, local copies, waits for them, and re-layouts, attend(): packed = jnp.dot(normed.reshape(-1, channels), qkv_w.reshape(channels, -1...  13.3 us
    dot_general x2, matrix products, attend(): jnp.einsum('bhqk,bkhe->bqhe', attn_prob, value_part, preferred_element_ty...  11.7 us
  transfers between devices with their start and end apart: 6, of which 6 were waited for; matrix products, arithmetic and copies ran while one was open for 3% of the time, Pallas kernels for 0%

commit v1 on v0

v1 whole, which is shorter than its diff:
```python
import functools

import jax
import jax.numpy as jnp
import numpy as np
from jax import lax
from jax.experimental import pallas as pl
from jax.experimental.pallas import tpu as pltpu
from jax.sharding import PartitionSpec as P

F32 = jnp.float32
BF = jnp.bfloat16
MESH = pl.DeviceIdType.MESH
HD = 64
GROUP = 4
SCALE = HD**-0.5 * 1.4426950408889634
STAGES = (("o", 0), ("q", 0), ("q", 1), ("q", 2), ("o", 1))


def layer_norm(v, gain):
    centred = v - jnp.mean(v, axis=-1, keepdims=True)
    spread = jnp.mean(centred * centred, axis=-1, keepdims=True)
    return (centred * lax.rsqrt(spread + 1e-06) * gain).astype(BF)


def attend(q, k, v, bias):
    rows = q.shape[0]
    lane = lax.broadcasted_iota(jnp.int32, (rows, 4 * HD), 1)
    low = lax.broadcasted_iota(jnp.int32, (rows, 2 * HD), 1) < HD
    keys = k.T
    none = jnp.zeros((HD, rows), BF)
    keys = jnp.concatenate(
        [
            jnp.concatenate([keys[HD * h : HD * h + HD] if g == h else none for g in range(GROUP)], axis=0)
            for h in range(GROUP)
        ],
        axis=1,
    )
    scores = jnp.dot(q, keys, preferred_element_type=F32)
    powers, scale = [], []
    for h in range(GROUP):
        s = scores[:, rows * h : rows * h + rows] * SCALE + bias
        e = jnp.exp2(s - jnp.max(s, axis=-1, keepdims=True))
        powers.append(e.astype(BF))
        scale.append(1.0 / jnp.sum(e, axis=-1, keepdims=True))
    empty = jnp.zeros((rows, 4 * HD), BF)
    values = jnp.concatenate(
        [jnp.where((lane >= HD * h) & (lane < HD * h + HD), v, empty) for h in range(GROUP)], axis=0
    )
    out = jnp.dot(jnp.concatenate(powers, axis=1), values, preferred_element_type=F32)
    left = out[:, : 2 * HD] * jnp.where(low, scale[0], scale[1])
    right = out[:, 2 * HD :] * jnp.where(low, scale[2], scale[3])
    return jnp.concatenate([left.astype(BF), right.astype(BF)], axis=1)


def kernel(
    counts, feats, wq_hbm, wo_hbm, gain, lscale, blend, out,
    wq, wo_own, wo_oth, x, nin, crop, qkv, heads, heads_in, heads2,
    upd_out, upd_in, fin_out, fin_in, bias,
    s_feat, s_wq, s_wo, s_out, h_send, h_recv, c_send, c_recv, u_send, u_recv, f_send, f_recv,
    x_send, x_recv, n_send, n_recv, b_send, b_recv,
):
    gy, gx, tp = lax.axis_index("gy"), lax.axis_index("gx"), lax.axis_index("tp")
    core, z, x_hi = gy % 2, (gy // 2) % 4, gy // 8
    dim = feats.shape[-1]
    tok = 256
    half = wo_hbm.shape[1]
    ng = half // 256

    def at_z(step):
        return (x_hi * 8 + ((z + step) % 4) * 2 + core, gx, tp)

    def at_y(step):
        return (gy, (gx + step) % 4, tp)

    twin = (gy + 1 - 2 * core, gx, tp)
    mate = (gy, gx, 1 - tp)
    mate_b = ((gy + 8) % 16, gx, 1 - tp)

    def remote(src, dst, ss, rs, dev):
        return pltpu.make_async_remote_copy(
            src_ref=src, dst_ref=dst, send_sem=ss, recv_sem=rs, device_id=dev, device_id_type=MESH
        )

    images = [3 * (1 - tp), 3 * tp, 1, 2]

    def quad(ref, image, t):
        return ref.at[image, pl.ds(8 * (t % 2), 8), pl.ds(8 * (t // 2), 8), :]

    def feat_copy(slot, t):
        return pltpu.make_async_copy(quad(feats, images[slot], t), x.at[slot, t], s_feat.at[slot, t])

    def out_copy(slot, t):
        return pltpu.make_async_copy(x.at[slot, t], quad(out, images[slot], t), s_out.at[slot, t])

    def wq_copy(layer, g):
        i = ng * layer + g
        return pltpu.make_async_copy(wq_hbm.at[layer, :, :, pl.ds(256 * g, 256)], wq.at[i], s_wq.at[i])

    def wo_copy(layer):
        return pltpu.make_async_copy(wo_hbm.at[layer], wo_own.at[layer], s_wo.at[layer])

    for t in range(4):
        feat_copy(0, t).start()
    for g in range(ng):
        wq_copy(0, g).start()

    barrier = pltpu.get_barrier_semaphore()

    def greet(dev):
        pl.semaphore_signal(barrier, inc=1, device_id=dev, device_id_type=MESH)

    for dev in (mate, mate_b, twin, at_z(1), at_z(-1), at_y(1), at_y(-1)):
        greet(dev)

    @pl.when(gy > 0)
    def _():
        greet((gy - 1, gx, tp))
        greet((gy - 1, (gx + 3) % 4, tp))

    @pl.when(gy < 15)
    def _():
        greet((gy + 1, gx, tp))
        greet((gy + 1, (gx + 1) % 4, tp))

    token = lax.broadcasted_iota(jnp.int32, (8, tok), 1)
    t_of, rr, cc = token // 64, (token % 64) // 8, token % 8

    def place(t):
        return (8 * (t % 2) + rr) * 16 + 8 * (t // 2) + cc

    bias[0] = jnp.where(place(t_of) < counts[gx, gy], 0.0, -1e30)
    below, right = jnp.minimum(gy + 1, 15), jnp.minimum(gx + 1, 3)
    in_y, in_x = gy < 15, gx < 3
    limit = jnp.full((8, tok), counts[gx, gy], jnp.int32)
    limit = jnp.where(t_of == 1, jnp.where(in_y, counts[gx, below], 0), limit)
    limit = jnp.where(t_of == 2, jnp.where(in_x, counts[right, gy], 0), limit)
    limit = jnp.where(t_of == 3, jnp.where(in_y & in_x, counts[right, below], 0), limit)
    bias[1] = jnp.where(place(3 - t_of) < limit, 0.0, -1e30)

    for slot in range(1, 4):
        for t in range(4):
            feat_copy(slot, t).start()
    wo_copy(0).start()

    @pl.when(gy == 0)
    def _():
        for k in range(3):
            upd_in[k, 0] = jnp.zeros((64, dim), BF)
            upd_in[k, 2] = jnp.zeros((64, dim), BF)

    @pl.when(gy == 15)
    def _():
        for k in range(3):
            crop[k, 64:128] = jnp.zeros((64, dim), BF)
            crop[k, 192:256] = jnp.zeros((64, dim), BF)

    pl.semaphore_wait(barrier, 7 + jnp.where(gy > 0, 2, 0) + jnp.where(gy < 15, 2, 0))

    def piece(s, col, part, rows_of):
        kind, idx = STAGES[s]
        depth = dim if kind == "q" else half
        per = depth // 8
        base = (col % 4) * (2 * per) + core * per
        size = per
        if part is not None:
            size = per // 2
            base = base + part * size
        rows = pl.ds(pl.multiple_of(base, 16), size)
        if kind == "q":
            if rows_of == "src":
                return wq_hbm.at[1, :, rows, pl.ds(256 * idx, 256)]
            return wq.at[2 * ng + idx, :, rows, :]
        if rows_of == "src":
            return wo_hbm.at[idx, rows, :]
        return wo_oth.at[idx, rows, :]

    def along_y(s):
        return s % 2 == 0

    def colour(s):
        return (gx + 2 * z) % 4 if along_y(s) else (z + 2 * gx) % 4

    def x_copies(s):
        col = colour(s)
        if s == 0:
            return [
                remote(piece(s, col, i, "src"), piece(s, col, i, "dst"), x_send.at[s, i], x_recv.at[s, i], dev)
                for i, dev in enumerate((mate, mate_b))
            ]
        return [remote(piece(s, col, None, "src"), piece(s, col, None, "dst"), x_send.at[s, 1], x_recv.at[s, 1], mate_b)]

    def n_copies(s, arriving=False):
        col = colour(s)
        near, far = (at_y, at_z) if along_y(s) else (at_z, at_y)
        plan = ((near(1), None, col - 1), (near(-1), None, col + 1), (far(1), 0, col + 2), (far(-1), 1, col + 2))
        res = []
        for i, (dev, part, other) in enumerate(plan):
            ref = piece(s, (other + 4) if arriving else col, part, "dst")
            res.append(remote(ref, ref, n_send.at[s, i], n_recv.at[s, i], dev))
        return res

    def b_copy(s, i):
        col = colour(s) + (0, 3, 1, 2)[i]
        ref = piece(s, col, None, "dst")
        return remote(ref, ref, b_send.at[s, i], b_recv.at[s, i], twin)

    def b_arrival(s, i):
        kind, idx = STAGES[s]
        depth = dim if kind == "q" else half
        per = depth // 8
        col = colour(s) + (0, 3, 1, 2)[i]
        rows = pl.ds(pl.multiple_of((col % 4) * (2 * per) + (1 - core) * per, 16), per)
        ref = wq.at[2 * ng + idx, :, rows, :] if kind == "q" else wo_oth.at[idx, rows, :]
        return remote(ref, ref, b_send.at[s, i], b_recv.at[s, i], twin)

    def first_hop(s):
        for c in x_copies(s):
            c.start()

    def second_hop(s):
        for c in x_copies(s):
            c.wait_recv()
        for c in n_copies(s):
            c.start()
        b_copy(s, 0).start()
        if s + 2 < len(STAGES):
            first_hop(s + 2)

    def third_hop(s):
        for c in n_copies(s, arriving=True):
            c.wait_recv()
        for i in (1, 2, 3):
            b_copy(s, i).start()

    def arrived(s):
        for i in range(4):
            b_arrival(s, i).wait_recv()

    first_hop(0)
    first_hop(1)
    for g in range(ng):
        wq_copy(1, g).start()
    wo_copy(1).start()

    def norm_into(slot, layer):
        for t in range(4):
            nin[slot, 64 * t : 64 * t + 64] = layer_norm(x[slot, t].reshape(64, dim), gain[layer : layer + 1, :])

    def project_in(n, w):
        return [jnp.dot(n, wq[w, j], preferred_element_type=F32).astype(BF) for j in range(3)]

    def keep(parts):
        for j in range(3):
            qkv[j] = parts[j]

    def heads_copy(idx, g):
        job = jnp.where(idx == 0, 0, idx + 1)
        return remote(heads.at[job, g], heads_in.at[idx, g], h_send.at[idx, g], h_recv.at[idx, g], mate)

    def feats_ready(slot):
        for t in range(4):
            feat_copy(slot, t).wait()

    feats_ready(0)
    norm_into(0, 0)
    for g in range(ng):
        wq_copy(0, g).wait()
    for slot in range(1, 4):
        feats_ready(slot)
    keep(project_in(nin[0], 0))

    steps = 4 * ng

    def first_step(i, carry):
        job, g = i // ng, i % ng

        @pl.when((g == 0) & (job < 3))
        def _():
            norm_into(job + 1, 0)

        later = jnp.minimum(i + 1, steps - 1)
        parts = project_in(nin[later // ng], later % ng)
        heads[job, g] = attend(qkv[0], qkv[1], qkv[2], bias[0, 0:1, :])
        keep(parts)

        @pl.when(job != 1)
        def _():
            heads_copy(jnp.where(job == 0, 0, job - 1), g).start()

        @pl.when(i == 2)
        def _():
            second_hop(0)

        @pl.when(i == 8)
        def _():
            third_hop(0)

        @pl.when(i == 9)
        def _():
            second_hop(1)

        return carry

    lax.fori_loop(0, steps, first_step, 0)

    def crop_copy(k, p):
        dev = (gy - (p % 2), (gx + 4 - p // 2) % 4, tp)
        return remote(
            nin.at[k + 1, pl.ds(64 * (3 - p), 64), :], crop.at[k, pl.ds(64 * p, 64), :],
            c_send.at[k, p - 1], c_recv.at[k, p - 1], dev,
        )

    def finish_first(k):
        for g in range(ng):
            heads_copy(k, g).wait_recv()
        own = jnp.concatenate([heads[k + 1, g] for g in range(ng)], axis=1)
        oth = jnp.concatenate([heads_in[k, g] for g in range(ng)], axis=1)

        def chunk(c, carry):
            cols = pl.ds(pl.multiple_of(c * 512, 512), 512)
            acc = jnp.dot(own, wo_own[0, :, cols], preferred_element_type=F32)
            acc = acc + jnp.dot(oth, wo_oth[0, :, cols], preferred_element_type=F32)
            acc = acc * lscale[0:1, cols]
            x[k + 1, :, :, :, cols] += acc.reshape(4, 8, 8, 512)
            if k == 0:
                fin_out[:, cols] = acc.astype(BF)
            return carry

        lax.fori_loop(0, dim // 512, chunk, 0)
        norm_into(k + 1, 1)
        crop_copy(k, 2).start()

        @pl.when(gy > 0)
        def _():
            crop_copy(k, 3).start()
            crop_copy(k, 1).start()

        crop[k, 0:64] = nin[k + 1, 192:256]

    wo_copy(0).wait()
    arrived(0)
    finish_first(0)
    third_hop(1)
    second_hop(2)
    finish_first(1)
    for g in range(ng):
        wq_copy(1, g).wait()
    wo_copy(1).wait()
    third_hop(2)
    second_hop(3)

    def upd_copy(k, p):
        dev = (gy + (p % 2), (gx + p // 2) % 4, tp)
        return remote(upd_out.at[k, p - 1], upd_in.at[k, 3 - p], u_send.at[k, p - 1], u_recv.at[k, p - 1], dev)

    def fin_copy(t):
        return remote(fin_out.at[pl.ds(64 * t, 64), :], fin_in.at[t], f_send.at[t], f_recv.at[t], mate)

    def crop_ready(k):
        crop_copy(k, 2).wait_recv()

        @pl.when(gy < 15)
        def _():
            crop_copy(k, 1).wait_recv()
            crop_copy(k, 3).wait_recv()

    def attend_crop(k):
        crop_ready(k)
        keep(project_in(crop[k], ng))

        def step(g, carry):
            if k == 0:

                @pl.when(g == 2)
                def _():
                    arrived(1)
                    finish_first(2)
                    third_hop(3)
                    second_hop(4)

                @pl.when(g == 3)
                def _():
                    arrived(2)

                @pl.when(g == 4)
                def _():
                    arrived(3)

            parts = project_in(crop[k], ng + g + 1)
            heads2[g] = attend(qkv[0], qkv[1], qkv[2], bias[1, 0:1, :])
            keep(parts)
            return carry

        lax.fori_loop(0, 2 * ng - 1, step, 0)
        heads2[2 * ng - 1] = attend(qkv[0], qkv[1], qkv[2], bias[1, 0:1, :])

    def project_crop(k):
        for lo in (128, 0):
            own = jnp.concatenate([heads2[g, lo : lo + 128] for g in range(ng)], axis=1)
            oth = jnp.concatenate([heads2[ng + g, lo : lo + 128] for g in range(ng)], axis=1)

            def chunk(c, carry, lo=lo, own=own, oth=oth):
                cols = pl.ds(pl.multiple_of(c * 512, 512), 512)
                acc = jnp.dot(own, wo_own[1, :, cols], preferred_element_type=F32)
                acc = acc + jnp.dot(oth, wo_oth[1, :, cols], preferred_element_type=F32)
                weight = jnp.concatenate([blend[lo : lo + 128]] * 4, axis=1)
                acc = acc * (lscale[1:2, cols] * weight)
                if lo == 0:
                    x[k + 1, 3, :, :, cols] += acc[:64].reshape(8, 8, 512)
                    upd_out[k, 0, :, cols] = acc[64:].astype(BF)
                    if k == 0:
                        fin_out[192:256, cols] = (fin_out[192:256, cols].astype(F32) + acc[:64]).astype(BF)
                else:
                    upd_out[k, 1, :, cols] = acc[:64].astype(BF)
                    upd_out[k, 2, :, cols] = acc[64:].astype(BF)
                return carry

            lax.fori_loop(0, dim // 512, chunk, 0)
            if lo == 128:
                upd_copy(k, 2).start()

                @pl.when(gy < 15)
                def _():
                    upd_copy(k, 3).start()
            else:

                @pl.when(gy < 15)
                def _():
                    upd_copy(k, 1).start()

                out_copy(k + 1, 3).start()
                if k == 0:
                    fin_copy(3).start()

    def blend_in(k):
        upd_copy(k, 2).wait_recv()

        @pl.when(gy > 0)
        def _():
            upd_copy(k, 1).wait_recv()
            upd_copy(k, 3).wait_recv()

        for t in (0, 1, 2):
            come = upd_in[k, t].astype(F32)
            if t < 2:
                come = jnp.where(gx > 0, come, 0.0)
            x[k + 1, t] += come.reshape(8, 8, dim)
            if k == 0:
                rows = slice(64 * t, 64 * t + 64)
                fin_out[rows] = (fin_out[rows].astype(F32) + come).astype(BF)
                fin_copy(t).start()
            out_copy(k + 1, t).start()

    attend_crop(0)
    third_hop(4)
    arrived(4)
    project_crop(0)
    attend_crop(1)
    project_crop(1)
    blend_in(0)
    attend_crop(2)
    project_crop(2)
    blend_in(1)
    for t in (3, 0, 1, 2):
        fin_copy(t).wait_recv()
        x[0, t] += fin_in[t].astype(F32).reshape(8, 8, dim)
        out_copy(0, t).start()
    blend_in(2)

    for s in range(len(STAGES)):
        for c in x_copies(s):
            c.wait_send()
        for c in n_copies(s):
            c.wait_send()
        for i in range(4):
            b_copy(s, i).wait_send()
    for k in range(3):
        for g in range(ng):
            heads_copy(k, g).wait_send()
        crop_copy(k, 2).wait_send()
        upd_copy(k, 2).wait_send()

        @pl.when(gy > 0)
        def _():
            crop_copy(k, 1).wait_send()
            crop_copy(k, 3).wait_send()

        @pl.when(gy < 15)
        def _():
            upd_copy(k, 1).wait_send()
            upd_copy(k, 3).wait_send()

    for t in range(4):
        fin_copy(t).wait_send()
        for slot in range(4):
            out_copy(slot, t).wait()


def blend_rows():
    token = np.arange(256)
    t, rr, cc = token // 64, (token % 64) // 8, token % 8
    r, c = 8 * (t % 2) + rr, 8 * (t // 2) + cc
    row = np.sin(np.pi * (r.astype(np.float32) + 0.5) / 16) ** 2
    col = np.sin(np.pi * (c.astype(np.float32) + 0.5) / 16) ** 2
    weight = (0.25 + 0.75 * row * col).astype(np.float32)
    return np.broadcast_to(weight[:, None], (256, 128)).copy()


def shards(features, qkv_weight, out_weight, norm_gain, layer_scale, valid_counts):
    dim = features.shape[-1]
    half = out_weight.shape[1]
    ng = half // 256
    anywhere = pl.BlockSpec(memory_space=pl.ANY)
    vmem = pl.BlockSpec(memory_space=pltpu.VMEM)
    dma = pltpu.SemaphoreType.DMA
    ns = len(STAGES)
    return pl.pallas_call(
        kernel,
        out_shape=jax.ShapeDtypeStruct(features.shape, F32),
        in_specs=[pl.BlockSpec(memory_space=pltpu.SMEM), anywhere, anywhere, anywhere, vmem, vmem, vmem],
        out_specs=anywhere,
        scratch_shapes=[
            pltpu.VMEM((3 * ng, 3, dim, 256), BF),
            pltpu.VMEM((2, half, dim), BF),
            pltpu.VMEM((2, half, dim), BF),
            pltpu.VMEM((4, 4, 8, 8, dim), F32),
            pltpu.VMEM((4, 256, dim), BF),
            pltpu.VMEM((3, 256, dim), BF),
            pltpu.VMEM((3, 256, 256), BF),
            pltpu.VMEM((4, ng, 256, 256), BF),
            pltpu.VMEM((3, ng, 256, 256), BF),
            pltpu.VMEM((2 * ng, 256, 256), BF),
            pltpu.VMEM((3, 3, 64, dim), BF),
            pltpu.VMEM((3, 3, 64, dim), BF),
            pltpu.VMEM((256, dim), BF),
            pltpu.VMEM((4, 64, dim), BF),
            pltpu.VMEM((2, 8, 256), F32),
            dma((4, 4)), dma((2 * ng,)), dma((2,)), dma((4, 4)),
            dma((3, ng)), dma((3, ng)), dma((3, 3)), dma((3, 3)), dma((3, 3)), dma((3, 3)), dma((4,)), dma((4,)),
            dma((ns, 2)), dma((ns, 2)), dma((ns, 4)), dma((ns, 4)), dma((ns, 4)), dma((ns, 4)),
        ],
        compiler_params=pltpu.CompilerParams(
            collective_id=0, has_side_effects=True, vmem_limit_bytes=60 * 2**20
        ),
        name="two_sublayers",
    )(
        valid_counts.T, features, jnp.transpose(qkv_weight, (0, 2, 1, 3)), out_weight,
        norm_gain, layer_scale, jnp.asarray(blend_rows()),
    )


def solution(mesh):
    in_specs = (
        P(None, "gy", "gx", None),
        P(None, None, None, "tp"),
        P(None, "tp", None),
        P(),
        P(),
        P(),
    )
    out_specs = P(None, "gy", "gx", None)
    return jax.shard_map(shards, mesh=mesh, in_specs=in_specs, out_specs=out_specs, check_vma=False)
```

time: 483 us -> 119 us (0.25)
  waiting for transfers between devices: 279 us -> 0 us
  Pallas kernels: 0 us -> 113 us
  local copies, waits for them, and re-layouts: 79.2 us -> 6.3 us
  other arithmetic: 51.5 us -> 0 us
  matrix products: 45.1 us -> 0 us
  between operations: 13.8 us -> 0.01 us
  starting transfers between devices: 11 us -> 0 us
    psum x2 -> x0, waiting for transfers between devices: 185 us -> none  [project(): return lax.psum(partial_out.astype(jnp.bfloat16), 'tp').astype(jnp.float32)]
    pallas_call x0 -> x1, Pallas kernels: none -> 113 us  [shards(): pl.pallas_call(kernel, out_shape=jax.ShapeDtypeStruct(features.shape, F32...]
    ppermute x4 -> x0, waiting for transfers between devices: 94.2 us -> none  [passed_along(): return lax.ppermute(block, axis, route)]
    dot_general x8 -> x0, matrix products: 45.1 us -> none  [the longest x2 21.2 us: attend(): jnp.dot(normed.reshape(-1, channels), qkv_w.reshape(channels, -1), prefer...]
    slice x8 -> x0, local copies, waits for them, and re-layouts: 19.4 us -> none  [the longest x1 10.1 us: shards(): qkv_weight[1]]
    reshape x2 -> x0, local copies, waits for them, and re-layouts: 17.7 us -> none  [attend(): packed = packed.reshape(images, length, 3, inner // HD, HD)]
    unnamed x30 -> x1, local copies, waits for them, and re-layouts: 22.9 us -> 6.3 us
    sub x2 -> x0, other arithmetic: 15.9 us -> none  [attend(): powers = jnp.exp(scores - largest)]
  transfers between devices with their start and end apart: 6 -> 0, of which waited for: 6 -> 0; matrix products, arithmetic and copies ran while one was open for 3% -> 0% of each run, Pallas kernels for 0% -> 0%
where the time goes in v1:
time: 119 us
  Pallas kernels  113 us (95%)
  local copies, waits for them, and re-layouts  6.3 us (5%)
    pallas_call x1, Pallas kernels, shards(): pl.pallas_call(kernel, out_shape=jax.ShapeDtypeStruct(features.shape, F32...  113 us
    unnamed x1, local copies, waits for them, and re-layouts  6.3 us

profile of v1, /device:TPU:6, one launch (start us, length us, event | category | flops | bytes accessed | tf_op | source)
XLA Modules:
  0.0 118.8 jit_solution(9758656393597839198)
XLA Ops:
  0.0 112.5 %two_sublayers.1 = f32[4,16,16,1536]{3,2,1,0:T(8,128)} custom-call(s32[4,16]{1,0:T(4,128)} %bitcast.3, f32[4,16,16,1536]{3,2,1,0:T(8,128)} %feats.1, bf16[2,3,1536,768]{3,2,1,0:T(8,128)(2,1)} %bitcast.2, bf16[2,768,1536]{2,1,0:T(8,128)(2,1)} %wo_hbm.1, f32[2,1536]{1,0:T(2,128)} %gain.1, f32[2,1536]{1,0:T(2,128)} %lscale.1, f32[256,128]{1,0:T(8,128)} %constant.2.clone.blend), custom_call_target="tpu_custom_call" | custom-call | tf_op jit(solution)/shard_map/two_sublayers/pallas_call | solution.py:518
  112.5 6.3 %copy.9 = f32[4,16,16,1536]{3,2,1,0:T(8,128)} copy(f32[4,16,16,1536]{3,2,1,0:T(8,128)} %two_sublayers.1) | data formatting | bytes 12582912

commit v2 on v1

--- a/solution.py
+++ b/solution.py
@@ -123,6 +123,21 @@
         greet((gy + 1, gx, tp))
         greet((gy + 1, (gx + 1) % 4, tp))
 
+    @pl.when(gy == 8)
+    def _():
+        greet((gy - 1, gx, 1 - tp))
+        greet((gy - 1, (gx + 3) % 4, 1 - tp))
+
+    @pl.when(gy == 7)
+    def _():
+        greet((gy + 1, gx, 1 - tp))
+        greet((gy + 1, (gx + 1) % 4, 1 - tp))
+
+    def side(k, p, edge):
+        if k == 0 or p == 2:
+            return tp
+        return jnp.where(gy == edge, 1 - tp, tp)
+
     token = lax.broadcasted_iota(jnp.int32, (8, tok), 1)
     t_of, rr, cc = token // 64, (token % 64) // 8, token % 8
 
@@ -155,7 +170,7 @@
             crop[k, 64:128] = jnp.zeros((64, dim), BF)
             crop[k, 192:256] = jnp.zeros((64, dim), BF)
 
-    pl.semaphore_wait(barrier, 7 + jnp.where(gy > 0, 2, 0) + jnp.where(gy < 15, 2, 0))
+    pl.semaphore_wait(barrier, 7 + jnp.where(gy > 0, 2, 0) + jnp.where(gy < 15, 2, 0) + jnp.where((gy == 7) | (gy == 8), 2, 0))
 
     def piece(s, col, part, rows_of):
         kind, idx = STAGES[s]
@@ -176,14 +191,14 @@
         return wo_oth.at[idx, rows, :]
 
     def along_y(s):
-        return s % 2 == 0
+        return s in (0, 2)
 
     def colour(s):
         return (gx + 2 * z) % 4 if along_y(s) else (z + 2 * gx) % 4
 
     def x_copies(s):
         col = colour(s)
-        if s == 0:
+        if s < 3:
             return [
                 remote(piece(s, col, i, "src"), piece(s, col, i, "dst"), x_send.at[s, i], x_recv.at[s, i], dev)
                 for i, dev in enumerate((mate, mate_b))
@@ -224,8 +239,6 @@
         for c in n_copies(s):
             c.start()
         b_copy(s, 0).start()
-        if s + 2 < len(STAGES):
-            first_hop(s + 2)
 
     def third_hop(s):
         for c in n_copies(s, arriving=True):
@@ -239,6 +252,7 @@
 
     first_hop(0)
     first_hop(1)
+    first_hop(2)
     for g in range(ng):
         wq_copy(1, g).start()
     wo_copy(1).start()
@@ -264,10 +278,7 @@
 
     feats_ready(0)
     norm_into(0, 0)
-    for g in range(ng):
-        wq_copy(0, g).wait()
-    for slot in range(1, 4):
-        feats_ready(slot)
+    wq_copy(0, 0).wait()
     keep(project_in(nin[0], 0))
 
     steps = 4 * ng
@@ -275,9 +286,18 @@
     def first_step(i, carry):
         job, g = i // ng, i % ng
 
-        @pl.when((g == 0) & (job < 3))
-        def _():
-            norm_into(job + 1, 0)
+        for slot in range(1, 4):
+
+            @pl.when(i == ng * (slot - 1))
+            def _(slot=slot):
+                feats_ready(slot)
+                norm_into(slot, 0)
+
+        for w in range(1, ng):
+
+            @pl.when(i == w - 1)
+            def _(w=w):
+                wq_copy(0, w).wait()
 
         later = jnp.minimum(i + 1, steps - 1)
         parts = project_in(nin[later // ng], later % ng)
@@ -292,20 +312,28 @@
         def _():
             second_hop(0)
 
+        @pl.when(i == 5)
+        def _():
+            second_hop(1)
+            first_hop(3)
+
+        @pl.when(i == 7)
+        def _():
+            third_hop(0)
+
         @pl.when(i == 8)
         def _():
-            third_hop(0)
-
-        @pl.when(i == 9)
-        def _():
-            second_hop(1)
+            second_hop(2)
+
+        @pl.when(i == 10)
+        def _():
+            third_hop(1)
+            first_hop(4)
 
         return carry
 
-    lax.fori_loop(0, steps, first_step, 0)
-
     def crop_copy(k, p):
-        dev = (gy - (p % 2), (gx + 4 - p // 2) % 4, tp)
+        dev = (gy - (p % 2), (gx + 4 - p // 2) % 4, side(k, p, 8))
         return remote(
             nin.at[k + 1, pl.ds(64 * (3 - p), 64), :], crop.at[k, pl.ds(64 * p, 64), :],
             c_send.at[k, p - 1], c_recv.at[k, p - 1], dev,
@@ -338,20 +366,21 @@
 
         crop[k, 0:64] = nin[k + 1, 192:256]
 
+    lax.fori_loop(0, steps, first_step, 0)
     wo_copy(0).wait()
     arrived(0)
     finish_first(0)
-    third_hop(1)
-    second_hop(2)
-    finish_first(1)
+    second_hop(3)
+    third_hop(2)
     for g in range(ng):
         wq_copy(1, g).wait()
     wo_copy(1).wait()
-    third_hop(2)
-    second_hop(3)
+    second_hop(4)
+    finish_first(1)
+    third_hop(3)
 
     def upd_copy(k, p):
-        dev = (gy + (p % 2), (gx + p // 2) % 4, tp)
+        dev = (gy + (p % 2), (gx + p // 2) % 4, side(k, p, 7))
         return remote(upd_out.at[k, p - 1], upd_in.at[k, 3 - p], u_send.at[k, p - 1], u_recv.at[k, p - 1], dev)
 
     def fin_copy(t):
@@ -375,12 +404,11 @@
                 @pl.when(g == 2)
                 def _():
                     arrived(1)
-                    finish_first(2)
-                    third_hop(3)
-                    second_hop(4)
 
                 @pl.when(g == 3)
                 def _():
+                    finish_first(2)
+                    third_hop(4)
                     arrived(2)
 
                 @pl.when(g == 4)
@@ -453,7 +481,6 @@
             out_copy(k + 1, t).start()
 
     attend_crop(0)
-    third_hop(4)
     arrived(4)
     project_crop(0)
     attend_crop(1)
@@ -507,6 +534,14 @@
     return np.broadcast_to(weight[:, None], (256, 128)).copy()
 
 
+def copy_kernel(src, dst, sems):
+    parts = [pltpu.make_async_copy(src.at[i], dst.at[i], sems.at[i]) for i in range(4)]
+    for c in parts:
+        c.start()
+    for c in parts:
+        c.wait()
+
+
 def shards(features, qkv_weight, out_weight, norm_gain, layer_scale, valid_counts):
     dim = features.shape[-1]
     half = out_weight.shape[1]
@@ -515,7 +550,7 @@
     vmem = pl.BlockSpec(memory_space=pltpu.VMEM)
     dma = pltpu.SemaphoreType.DMA
     ns = len(STAGES)
-    return pl.pallas_call(
+    result = pl.pallas_call(
         kernel,
         out_shape=jax.ShapeDtypeStruct(features.shape, F32),
         in_specs=[pl.BlockSpec(memory_space=pltpu.SMEM), anywhere, anywhere, anywhere, vmem, vmem, vmem],
@@ -548,6 +583,15 @@
         valid_counts.T, features, jnp.transpose(qkv_weight, (0, 2, 1, 3)), out_weight,
         norm_gain, layer_scale, jnp.asarray(blend_rows()),
     )
+    return pl.pallas_call(
+        copy_kernel,
+        out_shape=jax.ShapeDtypeStruct(features.shape, F32),
+        in_specs=[vmem],
+        out_specs=anywhere,
+        scratch_shapes=[dma((4,))],
+        compiler_params=pltpu.CompilerParams(vmem_limit_bytes=16 * 2**20),
+        name="result",
+    )(result)
 
 
 def solution(mesh):

time: 119 us -> 95.4 us (0.80)
  Pallas kernels: 113 us -> 92.5 us
  local copies, waits for them, and re-layouts: 6.3 us -> 2.78 us
    pallas_call x1, Pallas kernels: 113 us -> 89.8 us  [shards(): pl.pallas_call(kernel, out_shape=jax.ShapeDtypeStruct(features.shape, F32...]
    unnamed x1 -> x2, local copies, waits for them, and re-layouts: 6.3 us -> 2.78 us
    pallas_call x0 -> x1, Pallas kernels: none -> 2.73 us  [shards(): pl.pallas_call(copy_kernel, out_shape=jax.ShapeDtypeStruct(features.shape...]
where the time goes in v2:
time: 95.4 us; the launch traced here: 95.3 us
  Pallas kernels  92.5 us (97%)
  local copies, waits for them, and re-layouts  2.78 us (3%)
    pallas_call x1, Pallas kernels, shards(): pl.pallas_call(kernel, out_shape=jax.ShapeDtypeStruct(features.shape, F32...  89.8 us
    unnamed x2, local copies, waits for them, and re-layouts  2.78 us
    pallas_call x1, Pallas kernels, shards(): pl.pallas_call(copy_kernel, out_shape=jax.ShapeDtypeStruct(features.shape...  2.73 us

profile of v2, /device:TPU:6, one launch (start us, length us, event | category | flops | bytes accessed | tf_op | source)
XLA Modules:
  0.0 95.3 jit_solution(13260031331442836690)
XLA Ops:
  0.0 89.8 %two_sublayers.1.src = f32[4,16,16,1536]{3,2,1,0:T(8,128)} custom-call(s32[4,16]{1,0:T(4,128)} %bitcast.3, f32[4,16,16,1536]{3,2,1,0:T(8,128)} %feats.1, bf16[2,3,1536,768]{3,2,1,0:T(8,128)(2,1)} %bitcast.2, bf16[2,768,1536]{2,1,0:T(8,128)(2,1)} %wo_hbm.1, f32[2,1536]{1,0:T(2,128)} %gain.1, f32[2,1536]{1,0:T(2,128)} %lscale.1, f32[256,128]{1,0:T(8,128)} %constant.2.clone.blend), custom_call_target="tpu_custom_call" | custom-call | tf_op jit(solution)/shard_map/two_sublayers/pallas_call | solution.py:553
  89.8 0.0 copy-start
  89.8 2.8 %copy-done = f32[4,16,16,1536]{3,2,1,0:T(8,128)S(1)} copy-done((f32[4,16,16,1536]{3,2,1,0:T(8,128)S(1)}, f32[4,16,16,1536]{3,2,1,0:T(8,128)}, u32[]{:S(2)}) %copy-start) | copy-done | bytes 6291480
  92.5 2.7 %result.1 = f32[4,16,16,1536]{3,2,1,0:T(8,128)} custom-call(f32[4,16,16,1536]{3,2,1,0:T(8,128)S(1)} %copy-done), custom_call_target="tpu_custom_call" | custom-call | tf_op jit(solution)/shard_map/result/pallas_call | solution.py:586
Async XLA Ops:
  89.8 2.8 %copy-start = (f32[4,16,16,1536]{3,2,1,0:T(8,128)S(1)}, f32[4,16,16,1536]{3,2,1,0:T(8,128)}, u32[]{:S(2)}) copy-start(f32[4,16,16,1536]{3,2,1,0:T(8,128)} %two_sublayers.1.src) | copy-start | bytes 18874372

commit v3 on v2

--- a/solution.py
+++ b/solution.py
@@ -53,11 +53,20 @@
     return jnp.concatenate([left.astype(BF), right.astype(BF)], axis=1)
 
 
+def images_of(gy, tp):
+    pick = jnp.where(gy < 8, tp, 1 - tp)
+    return [3 * (1 - pick), 3 * pick, 1, 2]
+
+
+def quad(ref, image, t):
+    return ref.at[image, pl.ds(8 * (t % 2), 8), pl.ds(8 * (t // 2), 8), :]
+
+
 def kernel(
-    counts, feats, wq_hbm, wo_hbm, gain, lscale, blend, out,
-    wq, wo_own, wo_oth, x, nin, crop, qkv, heads, heads_in, heads2,
+    counts, feats, wq_hbm, wo_hbm, gain, lscale, blend, x,
+    wq, wo_own, wo_oth, nin, crop, qkv, heads, heads_in, heads2,
     upd_out, upd_in, fin_out, fin_in, bias,
-    s_feat, s_wq, s_wo, s_out, h_send, h_recv, c_send, c_recv, u_send, u_recv, f_send, f_recv,
+    s_feat, s_wq, s_wo, h_send, h_recv, c_send, c_recv, u_send, u_recv, f_send, f_recv,
     x_send, x_recv, n_send, n_recv, b_send, b_recv,
 ):
     gy, gx, tp = lax.axis_index("gy"), lax.axis_index("gx"), lax.axis_index("tp")
@@ -82,16 +91,10 @@
             src_ref=src, dst_ref=dst, send_sem=ss, recv_sem=rs, device_id=dev, device_id_type=MESH
         )
 
-    images = [3 * (1 - tp), 3 * tp, 1, 2]
-
-    def quad(ref, image, t):
-        return ref.at[image, pl.ds(8 * (t % 2), 8), pl.ds(8 * (t // 2), 8), :]
+    images = images_of(gy, tp)
 
     def feat_copy(slot, t):
         return pltpu.make_async_copy(quad(feats, images[slot], t), x.at[slot, t], s_feat.at[slot, t])
-
-    def out_copy(slot, t):
-        return pltpu.make_async_copy(x.at[slot, t], quad(out, images[slot], t), s_out.at[slot, t])
 
     def wq_copy(layer, g):
         i = ng * layer + g
@@ -133,8 +136,8 @@
         greet((gy + 1, gx, 1 - tp))
         greet((gy + 1, (gx + 1) % 4, 1 - tp))
 
-    def side(k, p, edge):
-        if k == 0 or p == 2:
+    def side(p, edge):
+        if p == 2:
             return tp
         return jnp.where(gy == edge, 1 - tp, tp)
 
@@ -257,8 +260,8 @@
         wq_copy(1, g).start()
     wo_copy(1).start()
 
-    def norm_into(slot, layer):
-        for t in range(4):
+    def norm_into(slot, layer, quarters=range(4)):
+        for t in quarters:
             nin[slot, 64 * t : 64 * t + 64] = layer_norm(x[slot, t].reshape(64, dim), gain[layer : layer + 1, :])
 
     def project_in(n, w):
@@ -333,7 +336,7 @@
         return carry
 
     def crop_copy(k, p):
-        dev = (gy - (p % 2), (gx + 4 - p // 2) % 4, side(k, p, 8))
+        dev = (gy - (p % 2), (gx + 4 - p // 2) % 4, side(p, 8))
         return remote(
             nin.at[k + 1, pl.ds(64 * (3 - p), 64), :], crop.at[k, pl.ds(64 * p, 64), :],
             c_send.at[k, p - 1], c_recv.at[k, p - 1], dev,
@@ -342,27 +345,34 @@
     def finish_first(k):
         for g in range(ng):
             heads_copy(k, g).wait_recv()
-        own = jnp.concatenate([heads[k + 1, g] for g in range(ng)], axis=1)
-        oth = jnp.concatenate([heads_in[k, g] for g in range(ng)], axis=1)
-
-        def chunk(c, carry):
-            cols = pl.ds(pl.multiple_of(c * 512, 512), 512)
-            acc = jnp.dot(own, wo_own[0, :, cols], preferred_element_type=F32)
-            acc = acc + jnp.dot(oth, wo_oth[0, :, cols], preferred_element_type=F32)
-            acc = acc * lscale[0:1, cols]
-            x[k + 1, :, :, :, cols] += acc.reshape(4, 8, 8, 512)
-            if k == 0:
-                fin_out[:, cols] = acc.astype(BF)
-            return carry
-
-        lax.fori_loop(0, dim // 512, chunk, 0)
-        norm_into(k + 1, 1)
-        crop_copy(k, 2).start()
-
-        @pl.when(gy > 0)
-        def _():
-            crop_copy(k, 3).start()
-            crop_copy(k, 1).start()
+        for lo in (0, 2):
+            rows = slice(64 * lo, 64 * lo + 128)
+            own = jnp.concatenate([heads[k + 1, g, rows] for g in range(ng)], axis=1)
+            oth = jnp.concatenate([heads_in[k, g, rows] for g in range(ng)], axis=1)
+
+            def chunk(c, carry, lo=lo, rows=rows, own=own, oth=oth):
+                cols = pl.ds(pl.multiple_of(c * 512, 512), 512)
+                acc = jnp.dot(own, wo_own[0, :, cols], preferred_element_type=F32)
+                acc = acc + jnp.dot(oth, wo_oth[0, :, cols], preferred_element_type=F32)
+                acc = acc * lscale[0:1, cols]
+                x[k + 1, lo : lo + 2, :, :, cols] += acc.reshape(2, 8, 8, 512)
+                if k == 0:
+                    fin_out[rows, cols] = acc.astype(BF)
+                return carry
+
+            lax.fori_loop(0, dim // 512, chunk, 0)
+            norm_into(k + 1, 1, (lo, lo + 1))
+            if lo == 0:
+                crop_copy(k, 2).start()
+
+                @pl.when(gy > 0)
+                def _():
+                    crop_copy(k, 3).start()
+            else:
+
+                @pl.when(gy > 0)
+                def _():
+                    crop_copy(k, 1).start()
 
         crop[k, 0:64] = nin[k + 1, 192:256]
 
@@ -380,7 +390,7 @@
     third_hop(3)
 
     def upd_copy(k, p):
-        dev = (gy + (p % 2), (gx + p // 2) % 4, side(k, p, 7))
+        dev = (gy + (p % 2), (gx + p // 2) % 4, side(p, 7))
         return remote(upd_out.at[k, p - 1], upd_in.at[k, 3 - p], u_send.at[k, p - 1], u_recv.at[k, p - 1], dev)
 
     def fin_copy(t):
@@ -457,7 +467,6 @@
                 def _():
                     upd_copy(k, 1).start()
 
-                out_copy(k + 1, 3).start()
                 if k == 0:
                     fin_copy(3).start()
 
@@ -478,7 +487,6 @@
                 rows = slice(64 * t, 64 * t + 64)
                 fin_out[rows] = (fin_out[rows].astype(F32) + come).astype(BF)
                 fin_copy(t).start()
-            out_copy(k + 1, t).start()
 
     attend_crop(0)
     arrived(4)
@@ -492,7 +500,6 @@
     for t in (3, 0, 1, 2):
         fin_copy(t).wait_recv()
         x[0, t] += fin_in[t].astype(F32).reshape(8, 8, dim)
-        out_copy(0, t).start()
     blend_in(2)
 
     for s in range(len(STAGES)):
@@ -520,8 +527,6 @@
 
     for t in range(4):
         fin_copy(t).wait_send()
-        for slot in range(4):
-            out_copy(slot, t).wait()
 
 
 def blend_rows():
@@ -535,7 +540,12 @@
 
 
 def copy_kernel(src, dst, sems):
-    parts = [pltpu.make_async_copy(src.at[i], dst.at[i], sems.at[i]) for i in range(4)]
+    images = images_of(lax.axis_index("gy"), lax.axis_index("tp"))
+    parts = [
+        pltpu.make_async_copy(src.at[slot, t], quad(dst, images[slot], t), sems.at[slot, t])
+        for slot in range(4)
+        for t in range(4)
+    ]
     for c in parts:
         c.start()
     for c in parts:
@@ -552,14 +562,13 @@
     ns = len(STAGES)
     result = pl.pallas_call(
         kernel,
-        out_shape=jax.ShapeDtypeStruct(features.shape, F32),
+        out_shape=pltpu.VMEM((4, 4, 8, 8, dim), F32),
         in_specs=[pl.BlockSpec(memory_space=pltpu.SMEM), anywhere, anywhere, anywhere, vmem, vmem, vmem],
-        out_specs=anywhere,
+        out_specs=vmem,
         scratch_shapes=[
             pltpu.VMEM((3 * ng, 3, dim, 256), BF),
             pltpu.VMEM((2, half, dim), BF),
             pltpu.VMEM((2, half, dim), BF),
-            pltpu.VMEM((4, 4, 8, 8, dim), F32),
             pltpu.VMEM((4, 256, dim), BF),
             pltpu.VMEM((3, 256, dim), BF),
             pltpu.VMEM((3, 256, 256), BF),
@@ -571,12 +580,12 @@
             pltpu.VMEM((256, dim), BF),
             pltpu.VMEM((4, 64, dim), BF),
             pltpu.VMEM((2, 8, 256), F32),
-            dma((4, 4)), dma((2 * ng,)), dma((2,)), dma((4, 4)),
+            dma((4, 4)), dma((2 * ng,)), dma((2,)),
             dma((3, ng)), dma((3, ng)), dma((3, 3)), dma((3, 3)), dma((3, 3)), dma((3, 3)), dma((4,)), dma((4,)),
             dma((ns, 2)), dma((ns, 2)), dma((ns, 4)), dma((ns, 4)), dma((ns, 4)), dma((ns, 4)),
         ],
         compiler_params=pltpu.CompilerParams(
-            collective_id=0, has_side_effects=True, vmem_limit_bytes=60 * 2**20
+            collective_id=0, has_side_effects=True, vmem_limit_bytes=54 * 2**20
         ),
         name="two_sublayers",
     )(
@@ -588,7 +597,7 @@
         out_shape=jax.ShapeDtypeStruct(features.shape, F32),
         in_specs=[vmem],
         out_specs=anywhere,
-        scratch_shapes=[dma((4,))],
+        scratch_shapes=[dma((4, 4))],
         compiler_params=pltpu.CompilerParams(vmem_limit_bytes=16 * 2**20),
         name="result",
     )(result)

time: 95.4 us -> 91.3 us (0.957)
  local copies, waits for them, and re-layouts: 2.78 us -> 0 us
  Pallas kernels: 92.5 us -> 90.5 us
    unnamed x2 -> x0, local copies, waits for them, and re-layouts: 2.78 us -> none
    pallas_call x1, Pallas kernels: 89.8 us -> 87.8 us  [shards(): pl.pallas_call(kernel, out_shape=pltpu.VMEM((4, 4, 8, 8, dim), F32), in_s...]
where the time goes in v3:
time: 91.3 us; the launch traced here: 90.7 us
  Pallas kernels  90.5 us (99%)
    pallas_call x1, Pallas kernels, shards(): pl.pallas_call(kernel, out_shape=pltpu.VMEM((4, 4, 8, 8, dim), F32), in_s...  87.8 us
    pallas_call x1, Pallas kernels, shards(): pl.pallas_call(copy_kernel, out_shape=jax.ShapeDtypeStruct(features.shape...  2.79 us

profile of v3, /device:TPU:6, one launch (start us, length us, event | category | flops | bytes accessed | tf_op | source)
XLA Modules:
  0.0 90.7 jit_solution(15277981387020671614)
XLA Ops:
  0.0 87.8 %two_sublayers.1.src = f32[4,4,8,8,1536]{4,3,2,1,0:T(8,128)S(1)} custom-call(s32[4,16]{1,0:T(4,128)} %bitcast.3, f32[4,16,16,1536]{3,2,1,0:T(8,128)} %feats.1, bf16[2,3,1536,768]{3,2,1,0:T(8,128)(2,1)} %bitcast.2, bf16[2,768,1536]{2,1,0:T(8,128)(2,1)} %wo_hbm.1, f32[2,1536]{1,0:T(2,128)} %gain.1, f32[2,1536]{1,0:T(2,128)} %lscale.1, ...), custom_call_target="tpu_custom_call" | custom-call | tf_op jit(solution)/shard_map/two_sublayers/pallas_call | solution.py:563
  87.8 2.8 %result.1 = f32[4,16,16,1536]{3,2,1,0:T(8,128)} custom-call(f32[4,4,8,8,1536]{4,3,2,1,0:T(8,128)S(1)} %two_sublayers.1.src), custom_call_target="tpu_custom_call" | custom-call | tf_op jit(solution)/shard_map/result/pallas_call | solution.py:595

commit v4 on v3

--- a/solution.py
+++ b/solution.py
@@ -256,9 +256,6 @@
     first_hop(0)
     first_hop(1)
     first_hop(2)
-    for g in range(ng):
-        wq_copy(1, g).start()
-    wo_copy(1).start()
 
     def norm_into(slot, layer, quarters=range(4)):
         for t in quarters:
@@ -314,6 +311,12 @@
         @pl.when(i == 2)
         def _():
             second_hop(0)
+
+        @pl.when(i == 4)
+        def _():
+            for w in range(ng):
+                wq_copy(1, w).start()
+            wo_copy(1).start()
 
         @pl.when(i == 5)
         def _():

time: 91.3 us -> 91.2 us (level)
  no operation moved by 1% of the time
where the time goes in v4:
time: 91.2 us; the launch traced here: 90.7 us
  Pallas kernels  90.6 us (99%)
    pallas_call x1, Pallas kernels, shards(): pl.pallas_call(kernel, out_shape=pltpu.VMEM((4, 4, 8, 8, dim), F32), in_s...  87.8 us
    pallas_call x1, Pallas kernels, shards(): pl.pallas_call(copy_kernel, out_shape=jax.ShapeDtypeStruct(features.shape...  2.79 us

profile of v4, /device:TPU:6, one launch (start us, length us, event | category | flops | bytes accessed | tf_op | source)
XLA Modules:
  0.0 90.7 jit_solution(17184377349917388440)
XLA Ops:
  0.0 87.8 %two_sublayers.1.src = f32[4,4,8,8,1536]{4,3,2,1,0:T(8,128)S(1)} custom-call(s32[4,16]{1,0:T(4,128)} %bitcast.3, f32[4,16,16,1536]{3,2,1,0:T(8,128)} %feats.1, bf16[2,3,1536,768]{3,2,1,0:T(8,128)(2,1)} %bitcast.2, bf16[2,768,1536]{2,1,0:T(8,128)(2,1)} %wo_hbm.1, f32[2,1536]{1,0:T(2,128)} %gain.1, f32[2,1536]{1,0:T(2,128)} %lscale.1, ...), custom_call_target="tpu_custom_call" | custom-call | tf_op jit(solution)/shard_map/two_sublayers/pallas_call | solution.py:566
  87.8 2.8 %result.1 = f32[4,16,16,1536]{3,2,1,0:T(8,128)} custom-call(f32[4,4,8,8,1536]{4,3,2,1,0:T(8,128)S(1)} %two_sublayers.1.src), custom_call_target="tpu_custom_call" | custom-call | tf_op jit(solution)/shard_map/result/pallas_call | solution.py:598
